TPU v7x, 128 devices: a whole 4x4x4 slice. The times are simulated.
128 devices in a mesh: section: 8 (over z_hi, y), ep: 16 (over x, z_lo, core).
Axes of the slice: x: 4, y: 4, z: 4 (z_hi: 2, z_lo: 2; z = z_hi * 2 + z_lo), core: 2. Of those that a mesh axis runs over, the one named last changes fastest.
Arguments:
- pending: bfloat16 [8, 2048, 7168], P('section', 'ep'), may hold values from -6 to 6
- expert_ids: int32 [8, 2048, 2], P('section', 'ep'), may hold values from 0 to 3, all different within a row; in each aligned block of 128 rows (0 to 127, 128 to 255, ..., all dimensions but the last counted through in order) at most 72 rows name the same one
- route_weight: float32 [8, 2048, 2], P('section', 'ep'), may hold values from 0.1 to 0.9
- gate_saved: bfloat16 [8, 1152, 4096], P('section', None, 'ep'), may hold values from -8 to 8
- up_saved: bfloat16 [8, 1152, 4096], P('section', None, 'ep'), may hold values from -8 to 8
- w_gate: bfloat16 [8, 7168, 4096], P('section', None, 'ep'), may hold values from -0.0625 to 0.0625
- w_up: bfloat16 [8, 7168, 4096], P('section', None, 'ep'), may hold values from -0.0625 to 0.0625
- w_down: bfloat16 [8, 4096, 7168], P('section', 'ep'), may hold values from -0.1875 to 0.1875
Outputs:
- upstream: bfloat16 [8, 2048, 7168], P('section', 'ep')
- down_grad: float32 [8, 4096, 7168], P('section', 'ep')
Inputs may be any that keep to these rules, and one draw needn't show every extreme that they name: `expert_ids`: each token names 2 different experts. In each aligned block of 128 tokens (the tokens of one device) no expert is named more than 72 times, and in every draw some block names some expert exactly 72 times.
All inputs are finite; a program needn't handle non-finite values.
Results may differ from a plain program's by a relative error of at most 0.006.
Values may be sent and summed in bfloat16 or wider, within the bound.
No kernel may reach another device: no remote copies, remote signals or barrier semaphores. Data moves between devices by JAX's collectives and lax.ppermute only.
A program may use at most 256 MiB of HBM per device.

v0:
```python
import jax
import jax.numpy as jnp
from jax import lax
from jax.sharding import PartitionSpec as P

SHARDS = 4


def from_behind(array, axis, by):
    peers = lax.axis_size(axis)
    return lax.ppermute(array, axis, [(i, (i + by) % peers) for i in range(peers)])


def expert_slots(rows, gate_part, up_part, w_gate, w_up, w_down):
    width = rows.shape[-1]
    hid = gate_part.shape[-1]
    flat = rows.reshape(-1, width)
    gate = gate_part.reshape(-1, hid).astype(jnp.float32)
    upval = up_part.reshape(-1, hid).astype(jnp.float32)
    sig = jax.nn.sigmoid(gate)
    slope = lax.dot_general(
        flat, w_down, (((1,), (1,)), ((), ())), preferred_element_type=jnp.float32
    )
    dgate = (slope * upval * sig * (1.0 + gate * (1.0 - sig))).astype(jnp.bfloat16)
    dupval = (slope * gate * sig).astype(jnp.bfloat16)
    hidden = (gate * sig * upval).astype(jnp.bfloat16)
    part = lax.dot_general(
        dgate, w_gate, (((1,), (1,)), ((), ())), preferred_element_type=jnp.float32
    )
    part = part + lax.dot_general(
        dupval, w_up, (((1,), (1,)), ((), ())), preferred_element_type=jnp.float32
    )
    grad_down = lax.dot_general(
        hidden, flat, (((0,), (0,)), ((), ())), preferred_element_type=jnp.float32
    )
    return (part.astype(jnp.bfloat16).reshape(rows.shape), grad_down)


def body(pending, expert_ids, route_weight, gate_saved, up_saved, w_gate, w_up, w_down):
    n_ep = lax.axis_size("ep")
    experts = n_ep // SHARDS
    own = pending[0]
    tok_count, width = own.shape
    topk = expert_ids.shape[2]
    cap = gate_saved.shape[1] // n_ep
    hid = gate_saved.shape[2]
    incoming = from_behind(own, "section", -1)
    ids = expert_ids[0].reshape(-1)
    probs = route_weight[0].reshape(-1)
    onehot = (ids[:, None] == jnp.arange(experts, dtype=jnp.int32)[None, :]).astype(jnp.int32)
    ranks = jnp.sum((jnp.cumsum(onehot, axis=0) - onehot) * onehot, axis=1)
    target = ids * cap + ranks
    scaled = (jnp.repeat(incoming.astype(jnp.float32), topk, axis=0) * probs[:, None]).astype(
        jnp.bfloat16
    )
    placer = (jnp.arange(experts * cap, dtype=jnp.int32)[:, None] == target[None, :]).astype(
        jnp.bfloat16
    )
    packed = jnp.dot(placer, scaled, preferred_element_type=jnp.float32).astype(jnp.bfloat16)
    copies = jnp.broadcast_to(
        packed.reshape(experts, 1, cap, width), (experts, SHARDS, cap, width)
    ).reshape(n_ep, cap, width)
    gate_rows = gate_saved[0].reshape(n_ep, cap, hid)
    up_rows = up_saved[0].reshape(n_ep, cap, hid)
    arrived = lax.all_to_all(copies, "ep", split_axis=0, concat_axis=0, tiled=True)
    part, grad_down = expert_slots(arrived, gate_rows, up_rows, w_gate[0], w_up[0], w_down[0])
    returned = lax.all_to_all(part, "ep", split_axis=0, concat_axis=0, tiled=True)
    summed = (
        returned.astype(jnp.float32)
        .reshape(experts, SHARDS, cap, width)
        .sum(axis=1)
        .reshape(experts * cap, width)
    )
    branch = (
        jnp.take(summed, target, axis=0)
        .reshape(tok_count, topk, width)
        .sum(axis=1)
        .astype(jnp.bfloat16)
    )
    kept = lax.optimization_barrier(branch).astype(jnp.float32)
    grad_in = (incoming.astype(jnp.float32) + kept).astype(jnp.bfloat16)
    upstream = from_behind(grad_in, "section", -1)
    return (upstream[None], grad_down[None])


def solution(mesh):
    placed = (
        P("section", "ep", None),
        P("section", "ep", None),
        P("section", "ep", None),
        P("section", None, "ep"),
        P("section", None, "ep"),
        P("section", None, "ep"),
        P("section", None, "ep"),
        P("section", "ep", None),
    )
    return jax.shard_map(
        body,
        mesh=mesh,
        in_specs=placed,
        out_specs=(P("section", "ep", None), P("section", "ep", None)),
        check_vma=False,
    )
```

profile of v0, /device:TPU:0, one launch (start us, length us, event | category | flops | bytes accessed | tf_op | source)
XLA Modules:
  0.0 668.7 jit_solution(8064669022139633647)
XLA Ops:
  0.6 6.5 collective-permute-start
  7.1 0.8 copy.19
  7.9 0.1 reshape_squeeze.3
  8.0 0.1 eq.39
  8.2 1.2 reduce-window.6
  9.4 0.1 slice.10
  9.5 0.1 copy.21
  9.6 0.1 copy.22
  9.7 0.8 copy.25
  10.5 0.1 mul.75
  10.7 0.1 add_bitcast_fusion
  10.8 35.9 %collective-permute-done = bf16[128,7168]{1,0:T(8,128)(2,1)S(1)} collective-permute-done((bf16[128,7168]{1,0:T(8,128)(2,1)}, bf16[128,7168]{1,0:T(8,128)(2,1)S(1)}, u32[]{:S(2)}, u32[]{:S(2)}) %collective-permute-start) | collective-permute-done | bytes 1835040 | tf_op jit(solution)/shard_map/ppermute | solution.py:11
  46.7 5.0 broadcast_in_dim.30
  51.7 9.6 %reshape.104 = f32[256,7168]{1,0:T(8,128)} reshape(f32[128,2,7168]{2,1,0:T(2,128)} %broadcast_in_dim.30) | data formatting | bytes 14680064 | tf_op jit(solution)/shard_map/reshape | solution.py:53
  61.2 4.4 convolution_convert_fusion
  65.6 2.0 broadcast_in_dim.32
  67.7 186.5 %all_to_all.10 = bf16[16,72,7168]{2,1,0:T(8,128)(2,1)S(1)} all-to-all(bf16[16,72,7168]{2,1,0:T(8,128)(2,1)S(1)} %bitcast.94), channel_id=1, replica_groups=mesh['section'=8,'ep'=16] {'ep'}, dimensions={0} | all-to-all | bytes 33030144 | tf_op jit(solution)/shard_map/all_to_all | solution.py:65
  254.2 0.0 copy-start
  254.2 5.7 copy-done
  259.8 0.0 copy-start.1
  259.8 0.0 copy-start.3
  259.8 6.8 %fusion.3 = f32[1152,256]{1,0:T(8,128)S(1)} fusion(bf16[1152,7168]{1,0:T(8,128)(2,1)S(1)} %bitcast.92, bf16[1,256,7168]{2,1,0:T(8,128)(2,1)} %param.15), kind=kOutput, calls=%fused_computation.10 | convolution fusion | flops 4227858432 | bytes 21364736 | tf_op jit(solution)/shard_map/dot_general | solution.py:21
  266.6 0.0 copy-start.2
  266.6 1.0 copy-done.2
  267.6 0.0 copy-done.1
  267.6 0.0 copy-done.3
  267.6 15.1 %fusion.1 = f32[1152,7168]{1,0:T(8,128)} fusion(bf16[1,7168,256]{2,1,0:T(8,128)(2,1)} %param.13, f32[1152,256]{1,0:T(8,128)S(1)} %fusion.3, bf16[1,1152,256]{2,1,0:T(8,128)(2,1)S(1)} %copy-done.3, bf16[1,1152,256]{2,1,0:T(8,128)(2,1)S(1)} %copy-done.1), kind=kOutput, calls=%fused_computation.8 | convolution fusion | flops 4231397376 | bytes 39059456 | tf_op jit(solution)/shard_map/dot_general | solution.py:27
  282.7 20.1 %add_convert_fusion = bf16[1152,7168]{1,0:T(8,128)(2,1)} fusion(f32[1152,7168]{1,0:T(8,128)} %fusion.1, bf16[1,7168,256]{2,1,0:T(8,128)(2,1)} %param.14, f32[1152,256]{1,0:T(8,128)} %copy-done.2, bf16[1,1152,256]{2,1,0:T(8,128)(2,1)S(1)} %copy-done.1), kind=kOutput, calls=%fused_computation.2 | convolution fusion | flops 4246437888 | bytes 54984704 | tf_op jit(solution)/shard_map/dot_general | solution.py:30
  302.8 0.0 copy-start.4
  302.8 5.5 all-to-all-start.1
  308.3 0.1 reduce_sum.32
  308.5 0.0 copy-done.4
  308.5 0.1 copy.26
  308.6 0.1 mul.84
  308.8 0.1 copy.23
  308.8 0.1 copy.24
  309.0 266.4 %all-to-all-done.1 = bf16[16,72,7168]{2,1,0:T(8,128)(2,1)} async-done(((bf16[16,72,7168]{2,1,0:T(8,128)(2,1)}), bf16[16,72,7168]{2,1,0:T(8,128)(2,1)}, u32[]{:S(2)}, u32[]{:S(2)}) %all-to-all-start.1) | async-done | bytes 16515104 | tf_op jit(solution)/shard_map/all_to_all | solution.py:67
  575.4 12.4 %convert_reduce_fusion = f32[4,72,7168]{2,1,0:T(8,128)} fusion(bf16[16,72,7168]{2,1,0:T(8,128)(2,1)} %all-to-all-done.1), kind=kLoop, calls=%fused_computation.1 | loop fusion | flops 14450688 | bytes 24772608 | tf_op jit(solution)/shard_map/reduce_sum | solution.py:71
  587.8 12.2 %gather_fusion = f32[256,7168]{1,0:T(8,128)} fusion(f32[288,7168]{1,0:T(8,128)} %bitcast.90, s32[1024]{0:T(1024)S(1)} %pad_clamp_fusion), kind=kCustom, calls=%fused_computation | custom fusion | bytes 14681088 | tf_op jit(solution)/shard_map/jit(_take)/gather | solution.py:75
  600.0 9.3 %gather.7 = f32[128,2,7168]{2,1,0:T(2,128)} reshape(f32[256,7168]{1,0:T(8,128)} %gather_fusion) | data formatting | bytes 14680064 | tf_op jit(solution)/shard_map/jit(_take)/gather | solution.py:75
  609.3 11.7 %select_reduce_fusion = bf16[128,7168]{1,0:T(8,128)(2,1)S(1)} fusion(f32[128,2,7168]{2,1,0:T(2,128)} %gather.7, pred[128,2]{1,0:T(8,128)(4,1)S(1)} %copy.24), kind=kLoop, calls=%fused_computation.5 | loop fusion | flops 2752512 | bytes 9175296 | tf_op jit(solution)/shard_map/reduce_sum | solution.py:77
  621.0 0.4 add_convert_fusion.1
  621.5 6.9 %collective-permute-start.1 = (bf16[128,7168]{1,0:T(8,128)(2,1)S(1)}, bf16[128,7168]{1,0:T(8,128)(2,1)S(1)}, u32[]{:S(2)}, u32[]{:S(2)}) collective-permute-start(bf16[128,7168]{1,0:T(8,128)(2,1)S(1)} %add_convert_fusion.1), channel_id=1, source_target_pairs={{0,112},{16,0},{32,16},{48,32},{64,48},{80,64},{96,80},{112,96},{1... | collective-permute-start | bytes 5505032 | tf_op jit(solution)/shard_map/ppermute | solution.py:11
  628.4 13.1 %convolution_bitcast_fusion = f32[1,256,7168]{2,1,0:T(8,128)} fusion(bf16[1152,7168]{1,0:T(8,128)(2,1)} %bitcast.93, bf16[1,1152,256]{2,1,0:T(8,128)(2,1)S(1)} %copy-done.3, bf16[1,1152,256]{2,1,0:T(8,128)(2,1)S(1)} %copy-done.1), kind=kOutput, calls=%fused_computation.3 | convolution fusion | flops 4230217728 | bytes 25034752 | tf_op jit(solution)/shard_map/dot_general | solution.py:33
  641.5 26.0 %collective-permute-done.1 = bf16[128,7168]{1,0:T(8,128)(2,1)S(1)} collective-permute-done((bf16[128,7168]{1,0:T(8,128)(2,1)S(1)}, bf16[128,7168]{1,0:T(8,128)(2,1)S(1)}, u32[]{:S(2)}, u32[]{:S(2)}) %collective-permute-start.1) | collective-permute-done | bytes 1835040 | tf_op jit(solution)/shard_map/ppermute | solution.py:11
  667.5 1.2 copy.30
  (9 shorter events, 0.1 us)
Async XLA Ops:
  0.6 46.1 %collective-permute-start = (bf16[128,7168]{1,0:T(8,128)(2,1)}, bf16[128,7168]{1,0:T(8,128)(2,1)S(1)}, u32[]{:S(2)}, u32[]{:S(2)}) collective-permute-start(bf16[128,7168]{1,0:T(8,128)(2,1)} %bitcast.100), channel_id=1, source_target_pairs={{0,112},{16,0},{32,16},{48,32},{64,48},{80,64},{96,80},{112,96},{1... | collective-permute-start | bytes 5505032 | tf_op jit(solution)/shard_map/ppermute | solution.py:11
  254.2 5.7 copy-start
  259.8 7.8 %copy-start.1 = (bf16[1,1152,256]{2,1,0:T(8,128)(2,1)S(1)}, bf16[1,1152,256]{2,1,0:T(8,128)(2,1)}, u32[]{:S(2)}) copy-start(bf16[1,1152,256]{2,1,0:T(8,128)(2,1)} %param.11) | copy-start | bytes 1769476
  259.8 7.8 %copy-start.3 = (bf16[1,1152,256]{2,1,0:T(8,128)(2,1)S(1)}, bf16[1,1152,256]{2,1,0:T(8,128)(2,1)}, u32[]{:S(2)}) copy-start(bf16[1,1152,256]{2,1,0:T(8,128)(2,1)} %param.12) | copy-start | bytes 1769476
  266.6 1.0 copy-start.2
  302.8 5.6 copy-start.4
  302.8 272.6 %all-to-all-start.1 = ((bf16[16,72,7168]{2,1,0:T(8,128)(2,1)}), bf16[16,72,7168]{2,1,0:T(8,128)(2,1)}, u32[]{:S(2)}, u32[]{:S(2)}) async-start(bf16[16,72,7168]{2,1,0:T(8,128)(2,1)} %bitcast.91), calls=%async_computation.1 | async-start | bytes 33030144 | tf_op jit(solution)/shard_map/all_to_all | solution.py:67
  621.5 46.0 %collective-permute-start.1 = (bf16[128,7168]{1,0:T(8,128)(2,1)S(1)}, bf16[128,7168]{1,0:T(8,128)(2,1)S(1)}, u32[]{:S(2)}, u32[]{:S(2)}) collective-permute-start(bf16[128,7168]{1,0:T(8,128)(2,1)S(1)} %add_convert_fusion.1), channel_id=1, source_target_pairs={{0,112},{16,0},{32,16},{48,32},{64,48},{80,64},{96,80},{112,96},{1... | collective-permute-start | bytes 5505032 | tf_op jit(solution)/shard_map/ppermute | solution.py:11
where the time goes:
time: 670 us; the launch traced here: 669 us
  waiting for transfers between devices  328 us (49%)
  blocking collectives  187 us (28%)
  matrix products  59.4 us (9%)
  local copies, waits for them, and re-layouts  48.8 us (7%)
  other arithmetic  26 us (4%)
  starting transfers between devices  18.9 us (3%)
    all_to_all x1, waiting for transfers between devices, body(): lax.all_to_all(part, 'ep', split_axis=0, concat_axis=0, tiled=True)  266 us
    all_to_all x1, blocking collectives, body(): lax.all_to_all(copies, 'ep', split_axis=0, concat_axis=0, tiled=True)  187 us
    ppermute x2, waiting for transfers between devices, from_behind(): lax.ppermute(array, axis, [(i, (i + by) % peers) for i in range(peers)])  62 us
    gather x2, local copies, waits for them, and re-layouts, body(): jnp.take(summed, target, axis=0).reshape(tok_count, topk, width).sum(axis=1)  21.5 us
    dot_general x1, matrix products, expert_slots(): lax.dot_general(dupval, w_up, (((1,), (1,)), ((), ())), preferred_element...  20.1 us
    dot_general x1, matrix products, expert_slots(): lax.dot_general(dgate, w_gate, (((1,), (1,)), ((), ())), preferred_elemen...  15.1 us
    ppermute x2, starting transfers between devices, from_behind(): lax.ppermute(array, axis, [(i, (i + by) % peers) for i in range(peers)])  13.4 us
  transfers between devices with their start and end apart: 3, of which 3 were waited for; matrix products, arithmetic and copies ran while one was open for 3% of the time, Pallas kernels for 0%

commit v1 on v0

v1 whole, which is shorter than its diff:
```python
import functools

import jax
import jax.numpy as jnp
from jax import lax
from jax.experimental import pallas as pl
from jax.experimental.pallas import tpu as pltpu
from jax.sharding import PartitionSpec as P

NX, NZ, NC = 4, 2, 2
F32, BF16 = jnp.float32, jnp.bfloat16
PARAMS = pltpu.CompilerParams(vmem_limit_bytes=40 << 20)
CHUNKS = (("B", 7), ("A", 7), ("B", 7), ("A", 7))
CONTRACT_LAST = (((1,), (1,)), ((), ()))


def section_move(array):
    peers = lax.axis_size("section")
    return lax.ppermute(array, "section", [(i, (i - 1) % peers) for i in range(peers)])


def ep_move(array, dx=0, dz=0, dc=0):
    pairs = []
    for q in range(NX * NZ * NC):
        x, z, c = q // (NZ * NC), q // NC % NZ, q % NC
        pairs.append((q, (x + dx) % NX * NZ * NC + (z ^ dz) * NC + (c ^ dc)))
    return lax.ppermute(array, "ep", pairs)


def whole(shape):
    return pl.BlockSpec(shape, lambda *_: (0,) * len(shape))


def tile_of(columns):
    return 256 if columns % 256 == 0 else 128


def route_kernel(cap, x_ref, info_ref, place_ref, place_t_ref, weight_ref):
    tokens = info_ref.shape[1]
    row = lax.broadcasted_iota(jnp.int32, (tokens, tokens), 0)
    col = lax.broadcasted_iota(jnp.int32, (tokens, tokens), 1)
    before = (row < col).astype(F32).astype(BF16)
    slot_of = lax.broadcasted_iota(jnp.int32, (cap, tokens), 0).astype(F32)
    places, weights = [], []
    for d in range(NX):
        expert = lax.rem(x_ref[0] + d, NX).astype(F32)
        first = info_ref[0:1, :] == expert
        second = info_ref[1:2, :] == expert
        named = jnp.where(first | second, 1.0, 0.0)
        prob = jnp.where(first, info_ref[2:3, :], jnp.where(second, info_ref[3:4, :], 0.0))
        rank = jnp.dot(
            jnp.broadcast_to(named, (8, tokens)).astype(BF16), before, preferred_element_type=F32
        )[0:1]
        placed = jnp.where((slot_of == rank) & (named > 0.0), 1.0, 0.0)
        places.append(placed)
        weights.append(
            jnp.broadcast_to(jnp.sum(placed * prob, axis=1, keepdims=True), (cap, 128))
        )
    place = jnp.concatenate(places, axis=0)
    place_ref[...] = place.astype(BF16)
    weight_ref[...] = jnp.concatenate(weights, axis=0)
    eye = (row == col).astype(F32).astype(BF16)
    place_t_ref[...] = lax.dot_general(
        eye, place.astype(BF16), CONTRACT_LAST, preferred_element_type=F32
    ).astype(BF16)


def route(x, info, cap):
    tokens = info.shape[1]
    slots = NX * cap
    return pl.pallas_call(
        functools.partial(route_kernel, cap),
        in_specs=[pl.BlockSpec(memory_space=pltpu.SMEM), whole(info.shape)],
        out_specs=[whole((slots, tokens)), whole((tokens, slots)), whole((slots, 128))],
        out_shape=[
            jax.ShapeDtypeStruct((slots, tokens), BF16),
            jax.ShapeDtypeStruct((tokens, slots), BF16),
            jax.ShapeDtypeStruct((slots, 128), F32),
        ],
        grid=(1,),
        compiler_params=PARAMS,
    )(x, info)


def saved_kernel(cap, at_ref, gate_ref, up_ref, f1_ref, f2_ref, ha_ref, hb_ref, g3, u3, h3):
    g3[...] = gate_ref[...].astype(F32).reshape(g3.shape)
    u3[...] = up_ref[...].astype(F32).reshape(u3.shape)
    x, z, c = at_ref[0], at_ref[1], at_ref[2]
    for cr in range(NC):
        for zr in range(NZ):
            for d in range(NX):
                j = (cr * NZ + zr) * NX + d
                jb = (cr * NX + d) * NZ + zr
                zs = z if zr == 0 else 1 - z
                cs = c if cr == 0 else 1 - c
                q = lax.rem(x + NX - d, NX) * (NZ * NC) + zs * NC + cs
                gate, upval = g3[q], u3[q]
                sig = jax.nn.sigmoid(gate)
                f1_ref[pl.ds(j * cap, cap), :] = upval * sig * (1.0 + gate * (1.0 - sig))
                f2_ref[pl.ds(j * cap, cap), :] = gate * sig
                h3[pl.ds(j * cap, cap), :] = gate * sig * upval
    ha_ref[...] = h3[...].astype(BF16)
    reorder_to_b(cap, h3, g3)
    hb_ref[...] = g3[...].reshape(hb_ref.shape).astype(BF16)


def reorder_to_b(cap, flat, blocks):
    for cr in range(NC):
        for zr in range(NZ):
            for d in range(NX):
                j = (cr * NZ + zr) * NX + d
                blocks[(cr * NX + d) * NZ + zr] = flat[pl.ds(j * cap, cap), :]


def saved(at, gate, up, cap):
    rows, hid = gate.shape
    blocks = rows // cap
    return pl.pallas_call(
        functools.partial(saved_kernel, cap),
        in_specs=[pl.BlockSpec(memory_space=pltpu.SMEM), whole(gate.shape), whole(up.shape)],
        out_specs=[whole((rows, hid))] * 4,
        out_shape=[jax.ShapeDtypeStruct((rows, hid), t) for t in (F32, F32, BF16, BF16)],
        scratch_shapes=[
            pltpu.VMEM((blocks, cap, hid), F32),
            pltpu.VMEM((blocks, cap, hid), F32),
            pltpu.VMEM((rows, hid), F32),
        ],
        grid=(1,),
        compiler_params=PARAMS,
    )(at, gate, up)


def pack_a_kernel(cap, place_ref, weight_ref, tok_ref, *outs):
    rows = jnp.dot(place_ref[...], tok_ref[...], preferred_element_type=F32)
    rows = rows * weight_ref[:, 0:1]
    for d in range(NX):
        outs[d][...] = rows[d * cap : (d + 1) * cap].astype(BF16)


def pack_a(place, weight, tok, cap):
    tokens, columns = tok.shape
    tile = tile_of(columns)
    return pl.pallas_call(
        functools.partial(pack_a_kernel, cap),
        in_specs=[
            whole(place.shape),
            whole(weight.shape),
            pl.BlockSpec((tokens, tile), lambda j: (0, j)),
        ],
        out_specs=[pl.BlockSpec((cap, tile), lambda j: (0, j))] * NX,
        out_shape=[jax.ShapeDtypeStruct((cap, columns), BF16)] * NX,
        grid=(columns // tile,),
        compiler_params=PARAMS,
    )(place, weight, tok)


def pack_b_kernel(cap, place0_ref, weight0_ref, place1_ref, weight1_ref, tok0_ref, tok1_ref, *outs):
    rows0 = jnp.dot(place0_ref[...], tok0_ref[...], preferred_element_type=F32)
    rows0 = rows0 * weight0_ref[:, 0:1]
    rows1 = jnp.dot(place1_ref[...], tok1_ref[...], preferred_element_type=F32)
    rows1 = rows1 * weight1_ref[:, 0:1]
    for d in range(NX):
        low, high = d * cap, (d + 1) * cap
        outs[d][...] = jnp.concatenate([rows0[low:high], rows1[low:high]], axis=0).astype(BF16)


def pack_b(place0, weight0, place1, weight1, tok0, tok1, cap):
    tokens, columns = tok0.shape
    tile = tile_of(columns)
    return pl.pallas_call(
        functools.partial(pack_b_kernel, cap),
        in_specs=[
            whole(place0.shape),
            whole(weight0.shape),
            whole(place1.shape),
            whole(weight1.shape),
            pl.BlockSpec((tokens, tile), lambda j: (0, j)),
            pl.BlockSpec((tokens, tile), lambda j: (0, j)),
        ],
        out_specs=[pl.BlockSpec((NZ * cap, tile), lambda j: (0, j))] * NX,
        out_shape=[jax.ShapeDtypeStruct((NZ * cap, columns), BF16)] * NX,
        grid=(columns // tile,),
        compiler_params=PARAMS,
    )(place0, weight0, place1, weight1, tok0, tok1)


def rows_kernel(groups, with_sum, with_grad, *refs):
    rows, refs = refs[:groups], refs[groups:]
    wd_ref, hid_ref = refs[:2]
    sum_in = refs[2] if with_sum else None
    sum_ref, grad_ref = refs[2 + with_sum + with_grad :]

    @pl.when(pl.program_id(0) == 0)
    def _():
        sum_ref[...] = jnp.zeros_like(sum_ref) if sum_in is None else sum_in[...]

    wd = wd_ref[...]
    grad = None
    for g in range(groups):
        block = rows[g][...]
        many = block.shape[0]
        sum_ref[pl.ds(g * many, many), :] += lax.dot_general(
            block, wd, CONTRACT_LAST, preferred_element_type=F32
        )
        more = jnp.dot(hid_ref[g], block, preferred_element_type=F32)
        grad = more if grad is None else grad + more
    grad_ref[...] = grad


def use_rows(rows, w_down, hid_t, dh, grad, start):
    groups = len(rows)
    many, columns = rows[0].shape
    hid, width = w_down.shape
    tile = tile_of(columns)
    first = start // tile
    at = pl.BlockSpec((hid, tile), lambda j: (0, first + j))
    operands = list(rows) + [w_down, hid_t]
    specs = [pl.BlockSpec((many, tile), lambda j: (0, j))] * groups + [at, whole(hid_t.shape)]
    aliases = {}
    if dh is not None:
        operands.append(dh)
        specs.append(whole(dh.shape))
    if grad is not None:
        aliases[len(operands)] = 1
        operands.append(grad)
        specs.append(pl.BlockSpec(memory_space=pl.ANY))
    return pl.pallas_call(
        functools.partial(rows_kernel, groups, dh is not None, grad is not None),
        in_specs=specs,
        out_specs=[whole((groups * many, hid)), at],
        out_shape=[
            jax.ShapeDtypeStruct((groups * many, hid), F32),
            jax.ShapeDtypeStruct((hid, width), F32),
        ],
        grid=(columns // tile,),
        input_output_aliases=aliases,
        compiler_params=PARAMS,
    )(*operands)


def act_kernel(cap, dha_ref, dhb_ref, f1_ref, f2_ref, ga_ref, ua_ref, gb_ref, ub_ref, flat, blocks):
    b3 = dhb_ref[...].reshape(blocks.shape)
    for cr in range(NC):
        for zr in range(NZ):
            for d in range(NX):
                j = (cr * NZ + zr) * NX + d
                here = pl.ds(j * cap, cap)
                flat[here, :] = dha_ref[here, :] + b3[(cr * NX + d) * NZ + zr]
    dh = flat[...]
    dgate = dh * f1_ref[...]
    dup = dh * f2_ref[...]
    ga_ref[...] = dgate.astype(BF16)
    ua_ref[...] = dup.astype(BF16)
    flat[...] = dgate
    reorder_to_b(cap, flat, blocks)
    gb_ref[...] = blocks[...].reshape(gb_ref.shape).astype(BF16)
    flat[...] = dup
    reorder_to_b(cap, flat, blocks)
    ub_ref[...] = blocks[...].reshape(ub_ref.shape).astype(BF16)


def activations(dha, dhb, f1, f2, cap):
    rows, hid = dha.shape
    return pl.pallas_call(
        functools.partial(act_kernel, cap),
        in_specs=[whole((rows, hid))] * 4,
        out_specs=[whole((rows, hid))] * 4,
        out_shape=[jax.ShapeDtypeStruct((rows, hid), BF16)] * 4,
        scratch_shapes=[
            pltpu.VMEM((rows, hid), F32),
            pltpu.VMEM((rows // cap, cap, hid), F32),
        ],
        grid=(1,),
        compiler_params=PARAMS,
    )(dha, dhb, f1, f2)


def part_kernel(pieces, with_other, dg_ref, du_ref, wg_ref, wu_ref, *refs):
    total = lax.dot_general(dg_ref[...], wg_ref[...], CONTRACT_LAST, preferred_element_type=F32)
    total += lax.dot_general(du_ref[...], wu_ref[...], CONTRACT_LAST, preferred_element_type=F32)
    if with_other:
        total += refs[0][...].astype(F32)
    outs = refs[with_other:]
    many = total.shape[0] // pieces
    for i in range(pieces):
        outs[i][...] = total[i * many : (i + 1) * many].astype(BF16)


def parts_of(dg, du, wg, wu, start, columns, half, other, pieces):
    rows, hid = dg.shape
    many = rows // NC
    tile = tile_of(columns)
    first = start // tile
    of_half = pl.BlockSpec((many, hid), lambda j: (half, 0))
    weights = pl.BlockSpec((tile, hid), lambda j: (first + j, 0))
    operands = [dg, du, wg, wu]
    specs = [of_half, of_half, weights, weights]
    if other is not None:
        operands.append(other)
        specs.append(pl.BlockSpec((many, tile), lambda j: (0, j)))
    return pl.pallas_call(
        functools.partial(part_kernel, pieces, other is not None),
        in_specs=specs,
        out_specs=[pl.BlockSpec((many // pieces, tile), lambda j: (0, j))] * pieces,
        out_shape=[jax.ShapeDtypeStruct((many // pieces, columns), BF16)] * pieces,
        grid=(columns // tile,),
        compiler_params=PARAMS,
    )(*operands)


def sum_z_kernel(cap, a_ref, b_ref, *outs):
    total = a_ref[...].astype(F32) + b_ref[...].astype(F32)
    for d in range(NX):
        outs[d][...] = total[d * cap : (d + 1) * cap].astype(BF16)


def sum_z(a, b, cap):
    rows, columns = a.shape
    tile = tile_of(columns)
    return pl.pallas_call(
        functools.partial(sum_z_kernel, cap),
        in_specs=[pl.BlockSpec((rows, tile), lambda j: (0, j))] * 2,
        out_specs=[pl.BlockSpec((cap, tile), lambda j: (0, j))] * NX,
        out_shape=[jax.ShapeDtypeStruct((cap, columns), BF16)] * NX,
        grid=(columns // tile,),
        compiler_params=PARAMS,
    )(a, b)


def finish_a_kernel(place_t_ref, tok_ref, *refs):
    blocks, out_ref = refs[:NX], refs[NX]
    rows = jnp.concatenate([b[...].astype(F32) for b in blocks], axis=0).astype(BF16)
    branch = jnp.dot(place_t_ref[...], rows, preferred_element_type=F32).astype(BF16)
    out_ref[...] = (tok_ref[...].astype(F32) + branch.astype(F32)).astype(BF16)


def finish_a(place_t, tok, blocks):
    tokens, columns = tok.shape
    cap = blocks[0].shape[0]
    tile = tile_of(columns)
    at = pl.BlockSpec((tokens, tile), lambda j: (0, j))
    return pl.pallas_call(
        finish_a_kernel,
        in_specs=[whole(place_t.shape), at]
        + [pl.BlockSpec((cap, tile), lambda j: (0, j))] * NX,
        out_specs=at,
        out_shape=jax.ShapeDtypeStruct((tokens, columns), BF16),
        grid=(columns // tile,),
        compiler_params=PARAMS,
    )(place_t, tok, *blocks)


def combine_b_kernel(cap, place0_ref, place1_ref, *refs):
    blocks, own_ref, other_ref = refs[:NX], refs[NX], refs[NX + 1]
    wide = [b[...].astype(F32) for b in blocks]
    for zr, (place_ref, out_ref) in enumerate(((place0_ref, own_ref), (place1_ref, other_ref))):
        rows = jnp.concatenate([b[zr * cap : (zr + 1) * cap] for b in wide], axis=0).astype(BF16)
        total = jnp.dot(place_ref[...], rows, preferred_element_type=F32)
        out_ref[...] = total.astype(out_ref.dtype)


def combine_b(place0_t, place1_t, blocks):
    tokens = place0_t.shape[0]
    many, columns = blocks[0].shape
    tile = tile_of(columns)
    at = pl.BlockSpec((tokens, tile), lambda j: (0, j))
    return pl.pallas_call(
        functools.partial(combine_b_kernel, many // NZ),
        in_specs=[whole(place0_t.shape), whole(place1_t.shape)]
        + [pl.BlockSpec((many, tile), lambda j: (0, j))] * NX,
        out_specs=[at, at],
        out_shape=[
            jax.ShapeDtypeStruct((tokens, columns), F32),
            jax.ShapeDtypeStruct((tokens, columns), BF16),
        ],
        grid=(columns // tile,),
        compiler_params=PARAMS,
    )(place0_t, place1_t, *blocks)


def finish_b_kernel(own_ref, other_ref, tok_ref, out_ref):
    branch = (own_ref[...] + other_ref[...].astype(F32)).astype(BF16)
    out_ref[...] = (tok_ref[...].astype(F32) + branch.astype(F32)).astype(BF16)


def finish_b(own, other, tok):
    tokens, columns = tok.shape
    tile = tile_of(columns)
    at = pl.BlockSpec((tokens, tile), lambda j: (0, j))
    return pl.pallas_call(
        finish_b_kernel,
        in_specs=[at, at, at],
        out_specs=at,
        out_shape=jax.ShapeDtypeStruct((tokens, columns), BF16),
        grid=(columns // tile,),
        compiler_params=PARAMS,
    )(own, other, tok)


def body(pending, expert_ids, route_weight, gate_saved, up_saved, w_gate, w_up, w_down):
    own = pending[0]
    width = own.shape[1]
    rows, hid = gate_saved.shape[1:]
    cap = rows // (NX * NZ * NC)
    w_gate, w_up, w_down = w_gate[0], w_up[0], w_down[0]
    chunks, start = [], 0
    for kind, size in CHUNKS:
        columns = size * width // 28
        chunks.append((kind, start, columns))
        start += columns

    incoming = [section_move(own[:, low : low + n]) for _, low, n in chunks]
    position = lax.axis_index("ep").astype(jnp.int32)
    x, z, c = position // (NZ * NC), position // NC % NZ, position % NC
    at = jnp.stack([x, z, c])
    info = jnp.concatenate([expert_ids[0].astype(F32), route_weight[0]], axis=1).T
    place0, place0_t, weight0 = route(at, info, cap)
    place1, place1_t, weight1 = route(at, ep_move(info, dz=1), cap)
    f1, f2, hid_a, hid_b = saved(at, gate_saved[0], up_saved[0], cap)
    hid_a = hid_a.reshape(NC * NZ, -1, hid).transpose(0, 2, 1)
    hid_b = hid_b.reshape(NC, -1, hid).transpose(0, 2, 1)

    dh = {"A": None, "B": None}
    grad = None
    for (kind, low, n), tok in zip(chunks, incoming):
        if kind == "A":
            sent = pack_a(place0, weight0, tok, cap)
            got = [sent[0]] + [ep_move(sent[d], dx=d) for d in range(1, NX)]
            near = jnp.concatenate(got, axis=0)
            far = ep_move(near, dz=1)
            groups = [near, far, ep_move(near, dc=1), ep_move(far, dc=1)]
            hid_t = hid_a
        else:
            across = ep_move(tok, dz=1)
            sent = pack_b(place0, weight0, place1, weight1, tok, across, cap)
            got = [sent[0]] + [ep_move(sent[d], dx=d) for d in range(1, NX)]
            near = jnp.concatenate(got, axis=0)
            groups = [near, ep_move(near, dc=1)]
            hid_t = hid_b
        dh[kind], grad = use_rows(groups, w_down, hid_t, dh[kind], grad, low)

    dg_a, du_a, dg_b, du_b = activations(dh["A"], dh["B"], f1, f2, cap)
    outs = []
    for (kind, low, n), tok in zip(chunks, incoming):
        dg, du = (dg_a, du_a) if kind == "A" else (dg_b, du_b)
        (theirs,) = parts_of(dg, du, w_gate, w_up, low, n, 1, None, 1)
        theirs = ep_move(theirs, dc=1)
        if kind == "A":
            keep, send = parts_of(dg, du, w_gate, w_up, low, n, 0, theirs, NZ)
            pieces = sum_z(keep, ep_move(send, dz=1), cap)
            got = [pieces[0]] + [ep_move(pieces[d], dx=-d) for d in range(1, NX)]
            done = finish_a(place0_t, tok, got)
        else:
            pieces = parts_of(dg, du, w_gate, w_up, low, n, 0, theirs, NX)
            got = [pieces[0]] + [ep_move(pieces[d], dx=-d) for d in range(1, NX)]
            mine, send = combine_b(place0_t, place1_t, got)
            done = finish_b(mine, ep_move(send, dz=1), tok)
        outs.append(section_move(done))
    return (jnp.concatenate(outs, axis=1)[None], grad[None])


def solution(mesh):
    placed = (
        P("section", "ep", None),
        P("section", "ep", None),
        P("section", "ep", None),
        P("section", None, "ep"),
        P("section", None, "ep"),
        P("section", None, "ep"),
        P("section", None, "ep"),
        P("section", "ep", None),
    )
    return jax.shard_map(
        body,
        mesh=mesh,
        in_specs=placed,
        out_specs=(P("section", "ep", None), P("section", "ep", None)),
        check_vma=False,
    )
```

time: 670 us -> 339 us (0.51)
  blocking collectives: 187 us -> 0 us
  waiting for transfers between devices: 328 us -> 149 us
  Pallas kernels: 0 us -> 87.4 us
  matrix products: 59.4 us -> 0 us
  starting transfers between devices: 18.9 us -> 71.3 us
  other arithmetic: 26 us -> 1.49 us
  local copies, waits for them, and re-layouts: 48.8 us -> 25.7 us
    all_to_all x1 -> x0, waiting for transfers between devices: 266 us -> none  [body(): lax.all_to_all(part, 'ep', split_axis=0, concat_axis=0, tiled=True)]
    all_to_all x1 -> x0, blocking collectives: 187 us -> none  [body(): lax.all_to_all(copies, 'ep', split_axis=0, concat_axis=0, tiled=True)]
    pallas_call x0 -> x28, Pallas kernels: none -> 87.4 us  [the longest x8 29.8 us: parts_of(): pl.pallas_call(functools.partial(part_kernel, pieces, other is not None),...]
    ppermute x2 -> x51, waiting for transfers between devices: 62 us -> 149 us  [the longest x43 103 us: ep_move(): return lax.ppermute(array, 'ep', pairs)]
    dot_general x5 -> x0, matrix products: 59.4 us -> none  [the longest x1 20.1 us: expert_slots(): lax.dot_general(dupval, w_up, (((1,), (1,)), ((), ())), preferred_element...]
    ppermute x2 -> x51, starting transfers between devices: 13.4 us -> 71.3 us  [the longest x43 46.3 us: ep_move(): return lax.ppermute(array, 'ep', pairs)]
    reduce_sum x3 -> x0, other arithmetic: 24.1 us -> none  [the longest x1 12.4 us: body(): summed = returned.astype(jnp.float32).reshape(experts, SHARDS, cap, width...]
    gather x2 -> x0, local copies, waits for them, and re-layouts: 21.5 us -> none  [body(): jnp.take(summed, target, axis=0).reshape(tok_count, topk, width).sum(axis=1)]
  transfers between devices with their start and end apart: 3 -> 51, of which waited for: 3 -> 23; matrix products, arithmetic and copies ran while one was open for 3% -> 3% of each run, Pallas kernels for 0% -> 22%
where the time goes in v1:
time: 339 us; the launch traced here: 336 us
  waiting for transfers between devices  149 us (44%)
  Pallas kernels  87.4 us (26%)
  starting transfers between devices  71.3 us (21%)
  local copies, waits for them, and re-layouts  25.7 us (8%)
    ppermute x43, waiting for transfers between devices, ep_move(): return lax.ppermute(array, 'ep', pairs)  103 us
    ppermute x43, starting transfers between devices, ep_move(): return lax.ppermute(array, 'ep', pairs)  46.3 us
    ppermute x8, waiting for transfers between devices, section_move(): lax.ppermute(array, 'section', [(i, (i - 1) % peers) for i in range(peers)])  46 us
    pallas_call x8, Pallas kernels, parts_of(): pl.pallas_call(functools.partial(part_kernel, pieces, other is not None),...  29.8 us
    pallas_call x4, Pallas kernels, use_rows(): pl.pallas_call(functools.partial(rows_kernel, groups, dh is not None, gra...  29.2 us
    ppermute x8, starting transfers between devices, section_move(): lax.ppermute(array, 'section', [(i, (i - 1) % peers) for i in range(peers)])  25 us
    unnamed x66, local copies, waits for them, and re-layouts  20.1 us
    pallas_call x2, Pallas kernels, combine_b(): pl.pallas_call(functools.partial(combine_b_kernel, many // NZ), in_specs=...  6.99 us
  transfers between devices with their start and end apart: 51, of which 23 were waited for; matrix products, arithmetic and copies ran while one was open for 3% of the time, Pallas kernels for 22%

profile of v1, /device:TPU:0, one launch (start us, length us, event | category | flops | bytes accessed | tf_op | source)
XLA Modules:
  0.0 335.8 jit_solution(5954100060937810807)
XLA Ops:
  0.6 1.6 fusion
  2.2 6.5 %collective-permute-start.8 = (bf16[128,1792]{1,0:T(8,128)(2,1)S(1)}, bf16[128,1792]{1,0:T(8,128)(2,1)S(1)}, u32[]{:S(2)}, u32[]{:S(2)}) collective-permute-start(bf16[128,1792]{1,0:T(8,128)(2,1)S(1)} %get-tuple-element.128), channel_id=1, source_target_pairs={{0,112},{16,0},{32,16},{48,32},{64,48},{80,64},{96,80},{112,96},{1... | collective-permute-start | bytes 1376264 | tf_op jit(solution)/shard_map/ppermute | solution.py:19
  14.6 5.1 %collective-permute-done.8.tok_ref = bf16[128,1792]{1,0:T(8,128)(2,1)S(1)} collective-permute-done((bf16[128,1792]{1,0:T(8,128)(2,1)S(1)}, bf16[128,1792]{1,0:T(8,128)(2,1)S(1)}, u32[]{:S(2)}, u32[]{:S(2)}) %collective-permute-start.8) | collective-permute-done | bytes 458784 | tf_op jit(solution)/shard_map/ppermute | solution.py:19
  19.6 1.5 shard_map.99
  21.1 1.6 collective-permute-start.9
  23.4 2.7 collective-permute-start.10
  26.1 3.3 collective-permute-done.1.tok_ref
  29.5 2.8 collective-permute-start.11
  32.2 1.5 shard_map.97
  35.2 4.1 %collective-permute-done.15.tok0_ref.tok_ref = bf16[128,1792]{1,0:T(8,128)(2,1)S(1)} collective-permute-done((bf16[128,1792]{1,0:T(8,128)(2,1)S(1)}, bf16[128,1792]{1,0:T(8,128)(2,1)S(1)}, u32[]{:S(2)}, u32[]{:S(2)}) %collective-permute-start.15) | collective-permute-done | bytes 458784 | tf_op jit(solution)/shard_map/ppermute | solution.py:19
  39.3 3.0 collective-permute-start.3
  44.1 4.0 %collective-permute-done.21.tok0_ref.tok_ref = bf16[128,1792]{1,0:T(8,128)(2,1)} collective-permute-done((bf16[128,1792]{1,0:T(8,128)(2,1)S(1)}, bf16[128,1792]{1,0:T(8,128)(2,1)}, u32[]{:S(2)}, u32[]{:S(2)}) %collective-permute-start.21) | collective-permute-done | bytes 458784 | tf_op jit(solution)/shard_map/ppermute | solution.py:19
  48.0 2.8 collective-permute-start.4
  52.5 1.9 shard_map.100
  54.5 1.7 collective-permute-start.17
  58.6 1.7 collective-permute-start.19
  60.3 1.8 collective-permute-done.22.tok1_ref
  62.1 4.4 %shard_map.103 = (bf16[144,1792]{1,0:T(8,128)(2,1)S(1)}, bf16[144,1792]{1,0:T(8,128)(2,1)S(1)}, bf16[144,1792]{1,0:T(8,128)(2,1)S(1)}, bf16[144,1792]{1,0:T(8,128)(2,1)S(1)}) custom-call(bf16[288,128]{1,0:T(8,128)(2,1)S(1)} %get-tuple-element.66.place_ref.place0_ref, f32[288,128]{1,0:T(8,128)S(1)} %get-tuple-element.67.weight_ref.weight0_ref, ...), custom_call_target="tpu_custom_call" | custom-call | tf_op jit(solution)/shard_map/pallas_call | solution.py:170
  67.2 12.9 %collective-permute-done.17 = bf16[144,1792]{1,0:T(8,128)(2,1)S(1)} collective-permute-done((bf16[144,1792]{1,0:T(8,128)(2,1)S(1)}, bf16[144,1792]{1,0:T(8,128)(2,1)S(1)}, u32[]{:S(2)}, u32[]{:S(2)}) %collective-permute-start.17) | collective-permute-done | bytes 516128 | tf_op jit(solution)/shard_map/ppermute | solution.py:27
  81.0 2.1 collective-permute-done.19
  84.1 16.9 %collective-permute-done.23 = bf16[144,1792]{1,0:T(8,128)(2,1)S(1)} collective-permute-done((bf16[144,1792]{1,0:T(8,128)(2,1)S(1)}, bf16[144,1792]{1,0:T(8,128)(2,1)S(1)}, u32[]{:S(2)}, u32[]{:S(2)}) %collective-permute-start.23) | collective-permute-done | bytes 516128 | tf_op jit(solution)/shard_map/ppermute | solution.py:27
  106.5 16.6 %collective-permute-done.12.refs_1_ = bf16[288,1792]{1,0:T(8,128)(2,1)} collective-permute-done((bf16[288,1792]{1,0:T(8,128)(2,1)}, bf16[288,1792]{1,0:T(8,128)(2,1)}, u32[]{:S(2)}, u32[]{:S(2)}) %collective-permute-start.12) | collective-permute-done | bytes 1032224 | tf_op jit(solution)/shard_map/ppermute | solution.py:27
  123.1 14.9 %collective-permute-done.5.refs_1_ = bf16[288,1792]{1,0:T(8,128)(2,1)} collective-permute-done((bf16[288,1792]{1,0:T(8,128)(2,1)}, bf16[288,1792]{1,0:T(8,128)(2,1)}, u32[]{:S(2)}, u32[]{:S(2)}) %collective-permute-start.5) | collective-permute-done | bytes 1032224 | tf_op jit(solution)/shard_map/ppermute | solution.py:27
  144.5 1.4 copy.13
  145.9 2.0 copy-done.2
  147.9 1.6 copy-done.7
  149.5 5.3 %shard_map.101 = (f32[1152,256]{1,0:T(8,128)S(1)}, f32[256,7168]{1,0:T(8,128)}) custom-call(bf16[576,1792]{1,0:T(8,128)(2,1)S(1)} %constant_dynamic-update-slice_fusion.8.refs_0_, bf16[576,1792]{1,0:T(8,128)(2,1)S(1)} %copy-done.7, bf16[256,7168]{1,0:T(8,128)(2,1)S(1)} %bitcast.37, bf16[2,256,576]{2,1,0:T(8,128)(2,1)S(1)} %bitcast.43), custom_call_target="tpu_custom_call" | custom-call | tf_op jit(solution)/shard_map/pallas_call | solution.py:227
  154.8 8.0 %shard_map.102 = (f32[1152,256]{1,0:T(8,128)S(1)}, f32[256,7168]{1,0:T(8,128)}) custom-call(bf16[288,1792]{1,0:T(8,128)(2,1)} %constant_dynamic-update-slice_fusion.4.refs_0_, bf16[288,1792]{1,0:T(8,128)(2,1)} %collective-permute-done.12.refs_1_, bf16[288,1792]{1,0:T(8,128)(2,1)} %collective-permute-done.13.refs_2_, ...), custom_call_target="tpu_custom_call", output_to_operand_aliasing={{1}: (6, {})} | custom-call | tf_op jit(solution)/shard_map/pallas_call | solution.py:227
  162.8 7.5 %shard_map.104 = (f32[1152,256]{1,0:T(8,128)S(1)}, f32[256,7168]{1,0:T(8,128)}) custom-call(bf16[576,1792]{1,0:T(8,128)(2,1)} %constant_dynamic-update-slice_fusion.12.refs_0_, bf16[576,1792]{1,0:T(8,128)(2,1)} %collective-permute-done.26.refs_1_, bf16[256,7168]{1,0:T(8,128)(2,1)S(1)} %bitcast.39, ...), custom_call_target="tpu_custom_call", output_to_operand_aliasing={{1}: (5, {})} | custom-call | tf_op jit(solution)/shard_map/pallas_call | solution.py:227
  170.4 8.4 %shard_map.105 = (f32[1152,256]{1,0:T(8,128)S(1)}, f32[256,7168]{1,0:T(8,128)}) custom-call(bf16[288,1792]{1,0:T(8,128)(2,1)} %constant_dynamic-update-slice_fusion.refs_0_, bf16[288,1792]{1,0:T(8,128)(2,1)} %collective-permute-done.5.refs_1_, bf16[288,1792]{1,0:T(8,128)(2,1)} %collective-permute-done.6.refs_2_, ...), custom_call_target="tpu_custom_call", output_to_operand_aliasing={{1}: (7, {})} | custom-call | tf_op jit(solution)/shard_map/pallas_call | solution.py:227
  179.1 1.7 copy-done
  180.8 4.4 %shard_map.107 = bf16[576,1792]{1,0:T(8,128)(2,1)} custom-call(bf16[1152,256]{1,0:T(8,128)(2,1)S(1)} %get-tuple-element.97.dg_ref, bf16[1152,256]{1,0:T(8,128)(2,1)S(1)} %get-tuple-element.98.du_ref, bf16[7168,256]{1,0:T(8,128)(2,1)S(1)} %bitcast.21, bf16[7168,256]{1,0:T(8,128)(2,1)S(1)} %bitcast.29), custom_call_target="tpu_custom_call" | custom-call | tf_op jit(solution)/shard_map/pallas_call | solution.py:301
  185.2 4.4 %shard_map.111 = bf16[576,1792]{1,0:T(8,128)(2,1)} custom-call(bf16[1152,256]{1,0:T(8,128)(2,1)S(1)} %get-tuple-element.105.dg_ref, bf16[1152,256]{1,0:T(8,128)(2,1)S(1)} %get-tuple-element.106.du_ref, bf16[7168,256]{1,0:T(8,128)(2,1)S(1)} %bitcast.22, bf16[7168,256]{1,0:T(8,128)(2,1)S(1)} %bitcast.30), custom_call_target="tpu_custom_call" | custom-call | tf_op jit(solution)/shard_map/pallas_call | solution.py:301
  190.1 4.4 %shard_map.119 = bf16[576,1792]{1,0:T(8,128)(2,1)} custom-call(bf16[1152,256]{1,0:T(8,128)(2,1)S(1)} %get-tuple-element.105.dg_ref, bf16[1152,256]{1,0:T(8,128)(2,1)S(1)} %get-tuple-element.106.du_ref, bf16[7168,256]{1,0:T(8,128)(2,1)S(1)} %bitcast.23, bf16[7168,256]{1,0:T(8,128)(2,1)S(1)} %bitcast.31), custom_call_target="tpu_custom_call" | custom-call | tf_op jit(solution)/shard_map/pallas_call | solution.py:301
  194.5 2.5 shard_map.115
  199.0 1.6 copy-done.5
  200.6 4.2 %shard_map.108 = (bf16[144,1792]{1,0:T(8,128)(2,1)S(1)}, bf16[144,1792]{1,0:T(8,128)(2,1)}, bf16[144,1792]{1,0:T(8,128)(2,1)S(1)}, bf16[144,1792]{1,0:T(8,128)(2,1)}) custom-call(bf16[1152,256]{1,0:T(8,128)(2,1)S(1)} %get-tuple-element.97.dg_ref, bf16[1152,256]{1,0:T(8,128)(2,1)S(1)} %get-tuple-element.98.du_ref, bf16[7168,256]{1,0:T(8,128)(2,1)S(1)} %bitcast.25, ...), custom_call_target="tpu_custom_call" | custom-call | tf_op jit(solution)/shard_map/pallas_call | solution.py:301
  205.2 1.7 collective-permute-start.30
  206.8 4.2 %shard_map.112 = (bf16[288,1792]{1,0:T(8,128)(2,1)S(1)}, bf16[288,1792]{1,0:T(8,128)(2,1)}) custom-call(bf16[1152,256]{1,0:T(8,128)(2,1)S(1)} %get-tuple-element.105.dg_ref, bf16[1152,256]{1,0:T(8,128)(2,1)S(1)} %get-tuple-element.106.du_ref, bf16[7168,256]{1,0:T(8,128)(2,1)S(1)} %bitcast.26, bf16[7168,256]{1,0:T(8,128)(2,1)S(1)} %bitcast.34, ...), custom_call_target="tpu_custom_call" | custom-call | tf_op jit(solution)/shard_map/pallas_call | solution.py:301
  212.0 2.8 shard_map.120
  215.9 2.8 shard_map.116
  219.7 1.8 collective-permute-start.40
  221.5 1.6 collective-permute-start.41
  223.1 8.9 %collective-permute-done.30.refs_3_ = bf16[144,1792]{1,0:T(8,128)(2,1)} collective-permute-done((bf16[144,1792]{1,0:T(8,128)(2,1)}, bf16[144,1792]{1,0:T(8,128)(2,1)}, u32[]{:S(2)}, u32[]{:S(2)}) %collective-permute-start.30) | collective-permute-done | bytes 516128 | tf_op jit(solution)/shard_map/ppermute | solution.py:27
  232.0 2.3 collective-permute-start.42
  234.4 5.0 %shard_map.109 = (f32[128,1792]{1,0:T(8,128)S(1)}, bf16[128,1792]{1,0:T(8,128)(2,1)S(1)}) custom-call(bf16[128,288]{1,0:T(8,128)(2,1)S(1)} %copy-done.15, bf16[128,288]{1,0:T(8,128)(2,1)S(1)} %copy-done.24, bf16[144,1792]{1,0:T(8,128)(2,1)S(1)} %get-tuple-element.99.refs_0_, bf16[144,1792]{1,0:T(8,128)(2,1)} %collective-permute-done.28.refs_1_, ...), custom_call_target="tpu_custom_call" | custom-call | tf_op jit(solution)/shard_map/pallas_call | solution.py:367
  239.3 2.4 collective-permute-done.40.refs_1_
  243.1 10.1 %collective-permute-done.42.refs_3_ = bf16[144,1792]{1,0:T(8,128)(2,1)S(1)} collective-permute-done((bf16[144,1792]{1,0:T(8,128)(2,1)S(1)}, bf16[144,1792]{1,0:T(8,128)(2,1)S(1)}, u32[]{:S(2)}, u32[]{:S(2)}) %collective-permute-start.42) | collective-permute-done | bytes 516128 | tf_op jit(solution)/shard_map/ppermute | solution.py:27
  253.2 2.0 shard_map.117
  257.0 1.4 collective-permute-start.35
  259.1 1.4 collective-permute-start.37
  261.2 7.7 %collective-permute-done.31.other_ref = bf16[128,1792]{1,0:T(8,128)(2,1)S(1)} collective-permute-done((bf16[128,1792]{1,0:T(8,128)(2,1)S(1)}, bf16[128,1792]{1,0:T(8,128)(2,1)S(1)}, u32[]{:S(2)}, u32[]{:S(2)}) %collective-permute-start.31) | collective-permute-done | bytes 458784 | tf_op jit(solution)/shard_map/ppermute | solution.py:27
  268.9 2.7 collective-permute-start.47
  271.6 5.6 %collective-permute-done.43.other_ref = bf16[128,1792]{1,0:T(8,128)(2,1)S(1)} collective-permute-done((bf16[128,1792]{1,0:T(8,128)(2,1)S(1)}, bf16[128,1792]{1,0:T(8,128)(2,1)S(1)}, u32[]{:S(2)}, u32[]{:S(2)}) %collective-permute-start.43) | collective-permute-done | bytes 458784 | tf_op jit(solution)/shard_map/ppermute | solution.py:27
  277.2 3.9 %collective-permute-start.48 = (bf16[72,1792]{1,0:T(8,128)(2,1)S(1)}, bf16[72,1792]{1,0:T(8,128)(2,1)S(1)}, u32[]{:S(2)}, u32[]{:S(2)}) collective-permute-start(bf16[72,1792]{1,0:T(8,128)(2,1)S(1)} %get-tuple-element.123), channel_id=1, source_target_pairs={{0,8},{1,9},{2,10},{3,11},{4,12},{5,13},{6,14},{7,15},{8,0},{9,1},... | collective-permute-start | bytes 774152 | tf_op jit(solution)/shard_map/ppermute | solution.py:27
  281.6 3.7 %shard_map.118 = bf16[128,1792]{1,0:T(8,128)(2,1)S(1)} custom-call(f32[128,1792]{1,0:T(8,128)S(1)} %get-tuple-element.117.own_ref, bf16[128,1792]{1,0:T(8,128)(2,1)S(1)} %collective-permute-done.43.other_ref, bf16[128,1792]{1,0:T(8,128)(2,1)} %collective-permute-done.21.tok0_ref.tok_ref), custom_call_target="tpu_custom_call" | custom-call | tf_op jit(solution)/shard_map/pallas_call | solution.py:390
  285.2 11.7 %collective-permute-start.32 = (bf16[128,1792]{1,0:T(8,128)(2,1)S(1)}, bf16[128,1792]{1,0:T(8,128)(2,1)S(1)}, u32[]{:S(2)}, u32[]{:S(2)}) collective-permute-start(bf16[128,1792]{1,0:T(8,128)(2,1)S(1)} %shard_map.110), channel_id=1, source_target_pairs={{0,112},{16,0},{32,16},{48,32},{64,48},{80,64},{96,80},{112,96},{1... | collective-permute-start | bytes 1376264 | tf_op jit(solution)/shard_map/ppermute | solution.py:19
  297.0 1.6 shard_map.114
  298.8 1.6 shard_map.122
  300.4 4.4 %collective-permute-start.50 = (bf16[128,1792]{1,0:T(8,128)(2,1)S(1)}, bf16[128,1792]{1,0:T(8,128)(2,1)S(1)}, u32[]{:S(2)}, u32[]{:S(2)}) collective-permute-start(bf16[128,1792]{1,0:T(8,128)(2,1)S(1)} %shard_map.122), channel_id=1, source_target_pairs={{0,112},{16,0},{32,16},{48,32},{64,48},{80,64},{96,80},{112,96},{1... | collective-permute-start | bytes 1376264 | tf_op jit(solution)/shard_map/ppermute | solution.py:19
  304.8 3.1 collective-permute-done.32
  307.9 9.8 %collective-permute-done.44 = bf16[128,1792]{1,0:T(8,128)(2,1)S(1)} collective-permute-done((bf16[128,1792]{1,0:T(8,128)(2,1)S(1)}, bf16[128,1792]{1,0:T(8,128)(2,1)S(1)}, u32[]{:S(2)}, u32[]{:S(2)}) %collective-permute-start.44) | collective-permute-done | bytes 458784 | tf_op jit(solution)/shard_map/ppermute | solution.py:19
  317.7 9.8 %collective-permute-done.38 = bf16[128,1792]{1,0:T(8,128)(2,1)S(1)} collective-permute-done((bf16[128,1792]{1,0:T(8,128)(2,1)S(1)}, bf16[128,1792]{1,0:T(8,128)(2,1)S(1)}, u32[]{:S(2)}, u32[]{:S(2)}) %collective-permute-start.38) | collective-permute-done | bytes 458784 | tf_op jit(solution)/shard_map/ppermute | solution.py:19
  327.6 6.8 %collective-permute-done.50 = bf16[128,1792]{1,0:T(8,128)(2,1)S(1)} collective-permute-done((bf16[128,1792]{1,0:T(8,128)(2,1)S(1)}, bf16[128,1792]{1,0:T(8,128)(2,1)S(1)}, u32[]{:S(2)}, u32[]{:S(2)}) %collective-permute-start.50) | collective-permute-done | bytes 458784 | tf_op jit(solution)/shard_map/ppermute | solution.py:19
  (143 shorter events, 41.0 us)
Async XLA Ops:
  0.6 8.8 %copy-start.25 = (s32[1,128,2]{1,2,0:T(2,128)S(1)}, s32[1,128,2]{1,2,0:T(2,128)}, u32[]{:S(2)}) copy-start(s32[1,128,2]{1,2,0:T(2,128)} %param.9) | copy-start | bytes 3076
  0.6 8.8 %copy-start.26 = (f32[1,128,2]{1,2,0:T(2,128)S(1)}, f32[1,128,2]{1,2,0:T(2,128)}, u32[]{:S(2)}) copy-start(f32[1,128,2]{1,2,0:T(2,128)} %param.10) | copy-start | bytes 3076
  2.2 17.4 %collective-permute-start.8 = (bf16[128,1792]{1,0:T(8,128)(2,1)S(1)}, bf16[128,1792]{1,0:T(8,128)(2,1)S(1)}, u32[]{:S(2)}, u32[]{:S(2)}) collective-permute-start(bf16[128,1792]{1,0:T(8,128)(2,1)S(1)} %get-tuple-element.128), channel_id=1, source_target_pairs={{0,112},{16,0},{32,16},{48,32},{64,48},{80,64},{96,80},{112,96},{1... | collective-permute-start | bytes 1376264 | tf_op jit(solution)/shard_map/ppermute | solution.py:19
  8.7 20.8 %collective-permute-start.1 = (bf16[128,1792]{1,0:T(8,128)(2,1)S(1)}, bf16[128,1792]{1,0:T(8,128)(2,1)S(1)}, u32[]{:S(2)}, u32[]{:S(2)}) collective-permute-start(bf16[128,1792]{1,0:T(8,128)(2,1)S(1)} %get-tuple-element.129), channel_id=1, source_target_pairs={{0,112},{16,0},{32,16},{48,32},{64,48},{80,64},{96,80},{112,96},{1... | collective-permute-start | bytes 1376264 | tf_op jit(solution)/shard_map/ppermute | solution.py:19
  9.5 4.2 %collective-permute-start = (f32[4,128]{1,0:T(4,128)S(1)}, f32[4,128]{1,0:T(4,128)S(1)}, u32[]{:S(2)}, u32[]{:S(2)}) collective-permute-start(f32[4,128]{1,0:T(4,128)S(1)} %maximum_bitcast_fusion.1.info_ref), channel_id=1, source_target_pairs={{0,2},{1,3},{2,0},{3,1},{4,6},{5,7},{6,4},{7,5},{8,10},{9,11},{10,... | collective-permute-start | bytes 6152 | tf_op jit(solution)/shard_map/ppermute | solution.py:27
  10.6 28.7 %collective-permute-start.15 = (bf16[128,1792]{1,0:T(8,128)(2,1)S(1)}, bf16[128,1792]{1,0:T(8,128)(2,1)S(1)}, u32[]{:S(2)}, u32[]{:S(2)}) collective-permute-start(bf16[128,1792]{1,0:T(8,128)(2,1)S(1)} %get-tuple-element.127), channel_id=1, source_target_pairs={{0,112},{16,0},{32,16},{48,32},{64,48},{80,64},{96,80},{112,96},{1... | collective-permute-start | bytes 1376264 | tf_op jit(solution)/shard_map/ppermute | solution.py:19
  11.6 36.4 %collective-permute-start.21 = (bf16[128,1792]{1,0:T(8,128)(2,1)S(1)}, bf16[128,1792]{1,0:T(8,128)(2,1)}, u32[]{:S(2)}, u32[]{:S(2)}) collective-permute-start(bf16[128,1792]{1,0:T(8,128)(2,1)S(1)} %get-tuple-element.126), channel_id=1, source_target_pairs={{0,112},{16,0},{32,16},{48,32},{64,48},{80,64},{96,80},{112,96},{1... | collective-permute-start | bytes 1376264 | tf_op jit(solution)/shard_map/ppermute | solution.py:19
  14.5 39.9 %copy-start.23 = (bf16[128,288]{1,0:T(8,128)(2,1)}, bf16[128,288]{1,0:T(8,128)(2,1)S(1)}, u32[]{:S(2)}) copy-start(bf16[128,288]{1,0:T(8,128)(2,1)S(1)} %get-tuple-element.65.place1_ref) | copy-start | bytes 221188
  19.6 34.8 %copy-start.10 = (bf16[128,1792]{1,0:T(8,128)(2,1)}, bf16[128,1792]{1,0:T(8,128)(2,1)S(1)}, u32[]{:S(2)}) copy-start(bf16[128,1792]{1,0:T(8,128)(2,1)S(1)} %collective-permute-done.8.tok_ref) | copy-start | bytes 1376260
  21.1 13.3 %collective-permute-start.9 = (bf16[72,1792]{1,0:T(8,128)(2,1)S(1)}, bf16[72,1792]{1,0:T(8,128)(2,1)S(1)}, u32[]{:S(2)}, u32[]{:S(2)}) collective-permute-start(bf16[72,1792]{1,0:T(8,128)(2,1)S(1)} %get-tuple-element.74), channel_id=1, source_target_pairs={{0,4},{1,5},{2,6},{3,7},{4,8},{5,9},{6,10},{7,11},{8,12},{9,13},{1... | collective-permute-start | bytes 774152 | tf_op jit(solution)/shard_map/ppermute | solution.py:27
  23.4 18.9 %collective-permute-start.10 = (bf16[72,1792]{1,0:T(8,128)(2,1)S(1)}, bf16[72,1792]{1,0:T(8,128)(2,1)S(1)}, u32[]{:S(2)}, u32[]{:S(2)}) collective-permute-start(bf16[72,1792]{1,0:T(8,128)(2,1)S(1)} %get-tuple-element.75), channel_id=1, source_target_pairs={{0,8},{1,9},{2,10},{3,11},{4,12},{5,13},{6,14},{7,15},{8,0},{9,1},... | collective-permute-start | bytes 774152 | tf_op jit(solution)/shard_map/ppermute | solution.py:27
  29.5 27.4 %copy-start.8 = (bf16[128,1792]{1,0:T(8,128)(2,1)}, bf16[128,1792]{1,0:T(8,128)(2,1)S(1)}, u32[]{:S(2)}) copy-start(bf16[128,1792]{1,0:T(8,128)(2,1)S(1)} %collective-permute-done.1.tok_ref) | copy-start | bytes 1376260
  29.5 21.3 %collective-permute-start.11 = (bf16[72,1792]{1,0:T(8,128)(2,1)S(1)}, bf16[72,1792]{1,0:T(8,128)(2,1)S(1)}, u32[]{:S(2)}, u32[]{:S(2)}) collective-permute-start(bf16[72,1792]{1,0:T(8,128)(2,1)S(1)} %get-tuple-element.76), channel_id=1, source_target_pairs={{0,12},{1,13},{2,14},{3,15},{4,0},{5,1},{6,2},{7,3},{8,4},{9,5},{1... | collective-permute-start | bytes 774152 | tf_op jit(solution)/shard_map/ppermute | solution.py:27
  34.5 21.7 %collective-permute-start.2 = (bf16[72,1792]{1,0:T(8,128)(2,1)S(1)}, bf16[72,1792]{1,0:T(8,128)(2,1)S(1)}, u32[]{:S(2)}, u32[]{:S(2)}) collective-permute-start(bf16[72,1792]{1,0:T(8,128)(2,1)S(1)} %get-tuple-element.69), channel_id=1, source_target_pairs={{0,4},{1,5},{2,6},{3,7},{4,8},{5,9},{6,10},{7,11},{8,12},{9,13},{1... | collective-permute-start | bytes 774152 | tf_op jit(solution)/shard_map/ppermute | solution.py:27
  39.3 21.0 %copy-start.12 = (bf16[128,1792]{1,0:T(8,128)(2,1)}, bf16[128,1792]{1,0:T(8,128)(2,1)S(1)}, u32[]{:S(2)}) copy-start(bf16[128,1792]{1,0:T(8,128)(2,1)S(1)} %collective-permute-done.15.tok0_ref.tok_ref) | copy-start | bytes 1376260
  39.3 18.6 %collective-permute-start.3 = (bf16[72,1792]{1,0:T(8,128)(2,1)S(1)}, bf16[72,1792]{1,0:T(8,128)(2,1)S(1)}, u32[]{:S(2)}, u32[]{:S(2)}) collective-permute-start(bf16[72,1792]{1,0:T(8,128)(2,1)S(1)} %get-tuple-element.70), channel_id=1, source_target_pairs={{0,8},{1,9},{2,10},{3,11},{4,12},{5,13},{6,14},{7,15},{8,0},{9,1},... | collective-permute-start | bytes 774152 | tf_op jit(solution)/shard_map/ppermute | solution.py:27
  42.3 10.2 %collective-permute-start.16 = (bf16[128,1792]{1,0:T(8,128)(2,1)S(1)}, bf16[128,1792]{1,0:T(8,128)(2,1)S(1)}, u32[]{:S(2)}, u32[]{:S(2)}) collective-permute-start(bf16[128,1792]{1,0:T(8,128)(2,1)S(1)} %collective-permute-done.15.tok0_ref.tok_ref), channel_id=1, source_target_pairs={{0,2},{1,3},{2,0},{3,1},{4,6},{5,7},{6,4},{7,5},{8,10},{9,11},{10,... | collective-permute-start | bytes 1376264 | tf_op jit(solution)/shard_map/ppermute | solution.py:27
  48.0 56.5 %collective-permute-start.4 = (bf16[72,1792]{1,0:T(8,128)(2,1)S(1)}, bf16[72,1792]{1,0:T(8,128)(2,1)S(1)}, u32[]{:S(2)}, u32[]{:S(2)}) collective-permute-start(bf16[72,1792]{1,0:T(8,128)(2,1)S(1)} %get-tuple-element.71), channel_id=1, source_target_pairs={{0,12},{1,13},{2,14},{3,15},{4,0},{5,1},{6,2},{7,3},{8,4},{9,5},{1... | collective-permute-start | bytes 774152 | tf_op jit(solution)/shard_map/ppermute | solution.py:27
  50.8 11.3 %collective-permute-start.22 = (bf16[128,1792]{1,0:T(8,128)(2,1)}, bf16[128,1792]{1,0:T(8,128)(2,1)S(1)}, u32[]{:S(2)}, u32[]{:S(2)}) collective-permute-start(bf16[128,1792]{1,0:T(8,128)(2,1)} %collective-permute-done.21.tok0_ref.tok_ref), channel_id=1, source_target_pairs={{0,2},{1,3},{2,0},{3,1},{4,6},{5,7},{6,4},{7,5},{8,10},{9,11},{10,... | collective-permute-start | bytes 1376264 | tf_op jit(solution)/shard_map/ppermute | solution.py:27
  54.5 25.7 %collective-permute-start.17 = (bf16[144,1792]{1,0:T(8,128)(2,1)S(1)}, bf16[144,1792]{1,0:T(8,128)(2,1)S(1)}, u32[]{:S(2)}, u32[]{:S(2)}) collective-permute-start(bf16[144,1792]{1,0:T(8,128)(2,1)S(1)} %get-tuple-element.80), channel_id=1, source_target_pairs={{0,4},{1,5},{2,6},{3,7},{4,8},{5,9},{6,10},{7,11},{8,12},{9,13},{1... | collective-permute-start | bytes 1548296 | tf_op jit(solution)/shard_map/ppermute | solution.py:27
  56.9 24.0 %collective-permute-start.18 = (bf16[144,1792]{1,0:T(8,128)(2,1)S(1)}, bf16[144,1792]{1,0:T(8,128)(2,1)S(1)}, u32[]{:S(2)}, u32[]{:S(2)}) collective-permute-start(bf16[144,1792]{1,0:T(8,128)(2,1)S(1)} %get-tuple-element.81), channel_id=1, source_target_pairs={{0,8},{1,9},{2,10},{3,11},{4,12},{5,13},{6,14},{7,15},{8,0},{9,1},... | collective-permute-start | bytes 1548296 | tf_op jit(solution)/shard_map/ppermute | solution.py:27
  58.6 24.5 %collective-permute-start.19 = (bf16[144,1792]{1,0:T(8,128)(2,1)S(1)}, bf16[144,1792]{1,0:T(8,128)(2,1)S(1)}, u32[]{:S(2)}, u32[]{:S(2)}) collective-permute-start(bf16[144,1792]{1,0:T(8,128)(2,1)S(1)} %get-tuple-element.82), channel_id=1, source_target_pairs={{0,12},{1,13},{2,14},{3,15},{4,0},{5,1},{6,2},{7,3},{8,4},{9,5},{1... | collective-permute-start | bytes 1548296 | tf_op jit(solution)/shard_map/ppermute | solution.py:27
  66.5 34.4 %collective-permute-start.23 = (bf16[144,1792]{1,0:T(8,128)(2,1)S(1)}, bf16[144,1792]{1,0:T(8,128)(2,1)S(1)}, u32[]{:S(2)}, u32[]{:S(2)}) collective-permute-start(bf16[144,1792]{1,0:T(8,128)(2,1)S(1)} %get-tuple-element.87), channel_id=1, source_target_pairs={{0,4},{1,5},{2,6},{3,7},{4,8},{5,9},{6,10},{7,11},{8,12},{9,13},{1... | collective-permute-start | bytes 1548296 | tf_op jit(solution)/shard_map/ppermute | solution.py:27
  80.2 22.7 %collective-permute-start.24 = (bf16[144,1792]{1,0:T(8,128)(2,1)S(1)}, bf16[144,1792]{1,0:T(8,128)(2,1)S(1)}, u32[]{:S(2)}, u32[]{:S(2)}) collective-permute-start(bf16[144,1792]{1,0:T(8,128)(2,1)S(1)} %get-tuple-element.88), channel_id=1, source_target_pairs={{0,8},{1,9},{2,10},{3,11},{4,12},{5,13},{6,14},{7,15},{8,0},{9,1},... | collective-permute-start | bytes 1548296 | tf_op jit(solution)/shard_map/ppermute | solution.py:27
  80.9 22.8 %collective-permute-start.25 = (bf16[144,1792]{1,0:T(8,128)(2,1)S(1)}, bf16[144,1792]{1,0:T(8,128)(2,1)S(1)}, u32[]{:S(2)}, u32[]{:S(2)}) collective-permute-start(bf16[144,1792]{1,0:T(8,128)(2,1)S(1)} %get-tuple-element.89), channel_id=1, source_target_pairs={{0,12},{1,13},{2,14},{3,15},{4,0},{5,1},{6,2},{7,3},{8,4},{9,5},{1... | collective-permute-start | bytes 1548296 | tf_op jit(solution)/shard_map/ppermute | solution.py:27
  83.1 54.9 %collective-permute-start.20 = (bf16[576,1792]{1,0:T(8,128)(2,1)S(1)}, bf16[576,1792]{1,0:T(8,128)(2,1)S(1)}, u32[]{:S(2)}, u32[]{:S(2)}) collective-permute-start(bf16[576,1792]{1,0:T(8,128)(2,1)S(1)} %constant_dynamic-update-slice_fusion.8.refs_0_), channel_id=1, source_target_pairs={{0,1},{1,0},{2,3},{3,2},{4,5},{5,4},{6,7},{7,6},{8,9},{9,8},{10,11... | collective-permute-start | bytes 6193160 | tf_op jit(solution)/shard_map/ppermute | solution.py:27
  84.0 55.8 %copy-start.20 = (bf16[1,1152,256]{2,1,0:T(8,128)(2,1)S(1)}, bf16[1,1152,256]{2,1,0:T(8,128)(2,1)}, u32[]{:S(2)}) copy-start(bf16[1,1152,256]{2,1,0:T(8,128)(2,1)} %param.11) | copy-start | bytes 1769476
  84.1 55.8 %copy-start.21 = (bf16[1,1152,256]{2,1,0:T(8,128)(2,1)S(1)}, bf16[1,1152,256]{2,1,0:T(8,128)(2,1)}, u32[]{:S(2)}) copy-start(bf16[1,1152,256]{2,1,0:T(8,128)(2,1)} %param.12) | copy-start | bytes 1769476
  101.0 22.1 %collective-permute-start.12 = (bf16[288,1792]{1,0:T(8,128)(2,1)}, bf16[288,1792]{1,0:T(8,128)(2,1)}, u32[]{:S(2)}, u32[]{:S(2)}) collective-permute-start(bf16[288,1792]{1,0:T(8,128)(2,1)} %constant_dynamic-update-slice_fusion.4.refs_0_), channel_id=1, source_target_pairs={{0,2},{1,3},{2,0},{3,1},{4,6},{5,7},{6,4},{7,5},{8,10},{9,11},{10,... | collective-permute-start | bytes 3096584 | tf_op jit(solution)/shard_map/ppermute | solution.py:27
  104.5 58.3 %collective-permute-start.26 = (bf16[576,1792]{1,0:T(8,128)(2,1)}, bf16[576,1792]{1,0:T(8,128)(2,1)}, u32[]{:S(2)}, u32[]{:S(2)}) collective-permute-start(bf16[576,1792]{1,0:T(8,128)(2,1)} %constant_dynamic-update-slice_fusion.12.refs_0_), channel_id=1, source_target_pairs={{0,1},{1,0},{2,3},{3,2},{4,5},{5,4},{6,7},{7,6},{8,9},{9,8},{10,11... | collective-permute-start | bytes 6193160 | tf_op jit(solution)/shard_map/ppermute | solution.py:27
  105.2 32.8 %collective-permute-start.5 = (bf16[288,1792]{1,0:T(8,128)(2,1)}, bf16[288,1792]{1,0:T(8,128)(2,1)}, u32[]{:S(2)}, u32[]{:S(2)}) collective-permute-start(bf16[288,1792]{1,0:T(8,128)(2,1)} %constant_dynamic-update-slice_fusion.refs_0_), channel_id=1, source_target_pairs={{0,2},{1,3},{2,0},{3,1},{4,6},{5,7},{6,4},{7,5},{8,10},{9,11},{10,... | collective-permute-start | bytes 3096584 | tf_op jit(solution)/shard_map/ppermute | solution.py:27
  106.3 48.5 %collective-permute-start.13 = (bf16[288,1792]{1,0:T(8,128)(2,1)}, bf16[288,1792]{1,0:T(8,128)(2,1)}, u32[]{:S(2)}, u32[]{:S(2)}) collective-permute-start(bf16[288,1792]{1,0:T(8,128)(2,1)} %constant_dynamic-update-slice_fusion.4.refs_0_), channel_id=1, source_target_pairs={{0,1},{1,0},{2,3},{3,2},{4,5},{5,4},{6,7},{7,6},{8,9},{9,8},{10,11... | collective-permute-start | bytes 3096584 | tf_op jit(solution)/shard_map/ppermute | solution.py:27
  123.1 31.7 %collective-permute-start.14 = (bf16[288,1792]{1,0:T(8,128)(2,1)}, bf16[288,1792]{1,0:T(8,128)(2,1)}, u32[]{:S(2)}, u32[]{:S(2)}) collective-permute-start(bf16[288,1792]{1,0:T(8,128)(2,1)} %collective-permute-done.12.refs_1_), channel_id=1, source_target_pairs={{0,1},{1,0},{2,3},{3,2},{4,5},{5,4},{6,7},{7,6},{8,9},{9,8},{10,11... | collective-permute-start | bytes 3096584 | tf_op jit(solution)/shard_map/ppermute | solution.py:27
  138.0 32.3 %collective-permute-start.6 = (bf16[288,1792]{1,0:T(8,128)(2,1)}, bf16[288,1792]{1,0:T(8,128)(2,1)}, u32[]{:S(2)}, u32[]{:S(2)}) collective-permute-start(bf16[288,1792]{1,0:T(8,128)(2,1)} %constant_dynamic-update-slice_fusion.refs_0_), channel_id=1, source_target_pairs={{0,1},{1,0},{2,3},{3,2},{4,5},{5,4},{6,7},{7,6},{8,9},{9,8},{10,11... | collective-permute-start | bytes 3096584 | tf_op jit(solution)/shard_map/ppermute | solution.py:27
  139.4 31.0 %collective-permute-start.7 = (bf16[288,1792]{1,0:T(8,128)(2,1)}, bf16[288,1792]{1,0:T(8,128)(2,1)}, u32[]{:S(2)}, u32[]{:S(2)}) collective-permute-start(bf16[288,1792]{1,0:T(8,128)(2,1)} %collective-permute-done.5.refs_1_), channel_id=1, source_target_pairs={{0,1},{1,0},{2,3},{3,2},{4,5},{5,4},{6,7},{7,6},{8,9},{9,8},{10,11... | collective-permute-start | bytes 3096584 | tf_op jit(solution)/shard_map/ppermute | solution.py:27
  185.2 12.4 %collective-permute-start.27 = (bf16[576,1792]{1,0:T(8,128)(2,1)}, bf16[576,1792]{1,0:T(8,128)(2,1)S(1)}, u32[]{:S(2)}, u32[]{:S(2)}) collective-permute-start(bf16[576,1792]{1,0:T(8,128)(2,1)} %shard_map.107), channel_id=1, source_target_pairs={{0,1},{1,0},{2,3},{3,2},{4,5},{5,4},{6,7},{7,6},{8,9},{9,8},{10,11... | collective-permute-start | bytes 6193160 | tf_op jit(solution)/shard_map/ppermute | solution.py:27
  189.6 15.6 %collective-permute-start.33 = (bf16[576,1792]{1,0:T(8,128)(2,1)}, bf16[576,1792]{1,0:T(8,128)(2,1)S(1)}, u32[]{:S(2)}, u32[]{:S(2)}) collective-permute-start(bf16[576,1792]{1,0:T(8,128)(2,1)} %shard_map.111), channel_id=1, source_target_pairs={{0,1},{1,0},{2,3},{3,2},{4,5},{5,4},{6,7},{7,6},{8,9},{9,8},{10,11... | collective-permute-start | bytes 6193160 | tf_op jit(solution)/shard_map/ppermute | solution.py:27
  194.5 16.5 %collective-permute-start.45 = (bf16[576,1792]{1,0:T(8,128)(2,1)}, bf16[576,1792]{1,0:T(8,128)(2,1)S(1)}, u32[]{:S(2)}, u32[]{:S(2)}) collective-permute-start(bf16[576,1792]{1,0:T(8,128)(2,1)} %shard_map.119), channel_id=1, source_target_pairs={{0,1},{1,0},{2,3},{3,2},{4,5},{5,4},{6,7},{7,6},{8,9},{9,8},{10,11... | collective-permute-start | bytes 6193160 | tf_op jit(solution)/shard_map/ppermute | solution.py:27
  197.1 17.7 %collective-permute-start.39 = (bf16[576,1792]{1,0:T(8,128)(2,1)S(1)}, bf16[576,1792]{1,0:T(8,128)(2,1)S(1)}, u32[]{:S(2)}, u32[]{:S(2)}) collective-permute-start(bf16[576,1792]{1,0:T(8,128)(2,1)S(1)} %shard_map.115), channel_id=1, source_target_pairs={{0,1},{1,0},{2,3},{3,2},{4,5},{5,4},{6,7},{7,6},{8,9},{9,8},{10,11... | collective-permute-start | bytes 6193160 | tf_op jit(solution)/shard_map/ppermute | solution.py:27
  204.8 14.9 %collective-permute-start.28 = (bf16[144,1792]{1,0:T(8,128)(2,1)}, bf16[144,1792]{1,0:T(8,128)(2,1)}, u32[]{:S(2)}, u32[]{:S(2)}) collective-permute-start(bf16[144,1792]{1,0:T(8,128)(2,1)} %get-tuple-element.100), channel_id=1, source_target_pairs={{0,12},{1,13},{2,14},{3,15},{4,0},{5,1},{6,2},{7,3},{8,4},{9,5},{1... | collective-permute-start | bytes 1548296 | tf_op jit(solution)/shard_map/ppermute | solution.py:27
  204.8 16.7 %collective-permute-start.29 = (bf16[144,1792]{1,0:T(8,128)(2,1)S(1)}, bf16[144,1792]{1,0:T(8,128)(2,1)}, u32[]{:S(2)}, u32[]{:S(2)}) collective-permute-start(bf16[144,1792]{1,0:T(8,128)(2,1)S(1)} %get-tuple-element.101), channel_id=1, source_target_pairs={{0,8},{1,9},{2,10},{3,11},{4,12},{5,13},{6,14},{7,15},{8,0},{9,1},... | collective-permute-start | bytes 1548296 | tf_op jit(solution)/shard_map/ppermute | solution.py:27
  205.2 26.9 %collective-permute-start.30 = (bf16[144,1792]{1,0:T(8,128)(2,1)}, bf16[144,1792]{1,0:T(8,128)(2,1)}, u32[]{:S(2)}, u32[]{:S(2)}) collective-permute-start(bf16[144,1792]{1,0:T(8,128)(2,1)} %get-tuple-element.102), channel_id=1, source_target_pairs={{0,4},{1,5},{2,6},{3,7},{4,8},{5,9},{6,10},{7,11},{8,12},{9,13},{1... | collective-permute-start | bytes 1548296 | tf_op jit(solution)/shard_map/ppermute | solution.py:27
  211.0 45.3 %collective-permute-start.34 = (bf16[288,1792]{1,0:T(8,128)(2,1)}, bf16[288,1792]{1,0:T(8,128)(2,1)S(1)}, u32[]{:S(2)}, u32[]{:S(2)}) collective-permute-start(bf16[288,1792]{1,0:T(8,128)(2,1)} %get-tuple-element.108), channel_id=1, source_target_pairs={{0,2},{1,3},{2,0},{3,1},{4,6},{5,7},{6,4},{7,5},{8,10},{9,11},{10,... | collective-permute-start | bytes 3096584 | tf_op jit(solution)/shard_map/ppermute | solution.py:27
  214.8 19.6 %copy-start.15 = (bf16[128,288]{1,0:T(8,128)(2,1)S(1)}, bf16[128,288]{1,0:T(8,128)(2,1)}, u32[]{:S(2)}) copy-start(bf16[128,288]{1,0:T(8,128)(2,1)} %copy-done.14) | copy-start | bytes 221188
  214.8 19.5 %copy-start.24 = (bf16[128,288]{1,0:T(8,128)(2,1)S(1)}, bf16[128,288]{1,0:T(8,128)(2,1)}, u32[]{:S(2)}) copy-start(bf16[128,288]{1,0:T(8,128)(2,1)} %copy-done.23) | copy-start | bytes 221188
  214.8 44.2 %collective-permute-start.46 = (bf16[288,1792]{1,0:T(8,128)(2,1)S(1)}, bf16[288,1792]{1,0:T(8,128)(2,1)S(1)}, u32[]{:S(2)}, u32[]{:S(2)}) collective-permute-start(bf16[288,1792]{1,0:T(8,128)(2,1)S(1)} %get-tuple-element.120), channel_id=1, source_target_pairs={{0,2},{1,3},{2,0},{3,1},{4,6},{5,7},{6,4},{7,5},{8,10},{9,11},{10,... | collective-permute-start | bytes 3096584 | tf_op jit(solution)/shard_map/ppermute | solution.py:27
  219.7 22.1 %collective-permute-start.40 = (bf16[144,1792]{1,0:T(8,128)(2,1)S(1)}, bf16[144,1792]{1,0:T(8,128)(2,1)S(1)}, u32[]{:S(2)}, u32[]{:S(2)}) collective-permute-start(bf16[144,1792]{1,0:T(8,128)(2,1)S(1)} %get-tuple-element.114), channel_id=1, source_target_pairs={{0,12},{1,13},{2,14},{3,15},{4,0},{5,1},{6,2},{7,3},{8,4},{9,5},{1... | collective-permute-start | bytes 1548296 | tf_op jit(solution)/shard_map/ppermute | solution.py:27
  221.5 21.6 %collective-permute-start.41 = (bf16[144,1792]{1,0:T(8,128)(2,1)S(1)}, bf16[144,1792]{1,0:T(8,128)(2,1)S(1)}, u32[]{:S(2)}, u32[]{:S(2)}) collective-permute-start(bf16[144,1792]{1,0:T(8,128)(2,1)S(1)} %get-tuple-element.115), channel_id=1, source_target_pairs={{0,8},{1,9},{2,10},{3,11},{4,12},{5,13},{6,14},{7,15},{8,0},{9,1},... | collective-permute-start | bytes 1548296 | tf_op jit(solution)/shard_map/ppermute | solution.py:27
  232.0 21.2 %collective-permute-start.42 = (bf16[144,1792]{1,0:T(8,128)(2,1)S(1)}, bf16[144,1792]{1,0:T(8,128)(2,1)S(1)}, u32[]{:S(2)}, u32[]{:S(2)}) collective-permute-start(bf16[144,1792]{1,0:T(8,128)(2,1)S(1)} %get-tuple-element.116), channel_id=1, source_target_pairs={{0,4},{1,5},{2,6},{3,7},{4,8},{5,9},{6,10},{7,11},{8,12},{9,13},{1... | collective-permute-start | bytes 1548296 | tf_op jit(solution)/shard_map/ppermute | solution.py:27
  241.8 27.1 %collective-permute-start.31 = (bf16[128,1792]{1,0:T(8,128)(2,1)S(1)}, bf16[128,1792]{1,0:T(8,128)(2,1)S(1)}, u32[]{:S(2)}, u32[]{:S(2)}) collective-permute-start(bf16[128,1792]{1,0:T(8,128)(2,1)S(1)} %get-tuple-element.104), channel_id=1, source_target_pairs={{0,2},{1,3},{2,0},{3,1},{4,6},{5,7},{6,4},{7,5},{8,10},{9,11},{10,... | collective-permute-start | bytes 1376264 | tf_op jit(solution)/shard_map/ppermute | solution.py:27
  255.2 21.9 %collective-permute-start.43 = (bf16[128,1792]{1,0:T(8,128)(2,1)S(1)}, bf16[128,1792]{1,0:T(8,128)(2,1)S(1)}, u32[]{:S(2)}, u32[]{:S(2)}) collective-permute-start(bf16[128,1792]{1,0:T(8,128)(2,1)S(1)} %get-tuple-element.118), channel_id=1, source_target_pairs={{0,2},{1,3},{2,0},{3,1},{4,6},{5,7},{6,4},{7,5},{8,10},{9,11},{10,... | collective-permute-start | bytes 1376264 | tf_op jit(solution)/shard_map/ppermute | solution.py:27
  256.3 24.7 %copy-start.13 = (bf16[128,1792]{1,0:T(8,128)(2,1)S(1)}, bf16[128,1792]{1,0:T(8,128)(2,1)}, u32[]{:S(2)}) copy-start(bf16[128,1792]{1,0:T(8,128)(2,1)} %copy-done.12) | copy-start | bytes 1376260
  257.0 24.0 %collective-permute-start.35 = (bf16[72,1792]{1,0:T(8,128)(2,1)S(1)}, bf16[72,1792]{1,0:T(8,128)(2,1)S(1)}, u32[]{:S(2)}, u32[]{:S(2)}) collective-permute-start(bf16[72,1792]{1,0:T(8,128)(2,1)S(1)} %get-tuple-element.110), channel_id=1, source_target_pairs={{0,12},{1,13},{2,14},{3,15},{4,0},{5,1},{6,2},{7,3},{8,4},{9,5},{1... | collective-permute-start | bytes 774152 | tf_op jit(solution)/shard_map/ppermute | solution.py:27
  258.4 26.8 %collective-permute-start.36 = (bf16[72,1792]{1,0:T(8,128)(2,1)S(1)}, bf16[72,1792]{1,0:T(8,128)(2,1)S(1)}, u32[]{:S(2)}, u32[]{:S(2)}) collective-permute-start(bf16[72,1792]{1,0:T(8,128)(2,1)S(1)} %get-tuple-element.111), channel_id=1, source_target_pairs={{0,8},{1,9},{2,10},{3,11},{4,12},{5,13},{6,14},{7,15},{8,0},{9,1},... | collective-permute-start | bytes 774152 | tf_op jit(solution)/shard_map/ppermute | solution.py:27
  259.1 37.9 %collective-permute-start.37 = (bf16[72,1792]{1,0:T(8,128)(2,1)S(1)}, bf16[72,1792]{1,0:T(8,128)(2,1)S(1)}, u32[]{:S(2)}, u32[]{:S(2)}) collective-permute-start(bf16[72,1792]{1,0:T(8,128)(2,1)S(1)} %get-tuple-element.112), channel_id=1, source_target_pairs={{0,4},{1,5},{2,6},{3,7},{4,8},{5,9},{6,10},{7,11},{8,12},{9,13},{1... | collective-permute-start | bytes 774152 | tf_op jit(solution)/shard_map/ppermute | solution.py:27
  268.9 29.8 %collective-permute-start.47 = (bf16[72,1792]{1,0:T(8,128)(2,1)S(1)}, bf16[72,1792]{1,0:T(8,128)(2,1)S(1)}, u32[]{:S(2)}, u32[]{:S(2)}) collective-permute-start(bf16[72,1792]{1,0:T(8,128)(2,1)S(1)} %get-tuple-element.122), channel_id=1, source_target_pairs={{0,12},{1,13},{2,14},{3,15},{4,0},{5,1},{6,2},{7,3},{8,4},{9,5},{1... | collective-permute-start | bytes 774152 | tf_op jit(solution)/shard_map/ppermute | solution.py:27
  277.2 21.6 %collective-permute-start.48 = (bf16[72,1792]{1,0:T(8,128)(2,1)S(1)}, bf16[72,1792]{1,0:T(8,128)(2,1)S(1)}, u32[]{:S(2)}, u32[]{:S(2)}) collective-permute-start(bf16[72,1792]{1,0:T(8,128)(2,1)S(1)} %get-tuple-element.123), channel_id=1, source_target_pairs={{0,8},{1,9},{2,10},{3,11},{4,12},{5,13},{6,14},{7,15},{8,0},{9,1},... | collective-permute-start | bytes 774152 | tf_op jit(solution)/shard_map/ppermute | solution.py:27
  281.0 17.8 %collective-permute-start.49 = (bf16[72,1792]{1,0:T(8,128)(2,1)S(1)}, bf16[72,1792]{1,0:T(8,128)(2,1)S(1)}, u32[]{:S(2)}, u32[]{:S(2)}) collective-permute-start(bf16[72,1792]{1,0:T(8,128)(2,1)S(1)} %get-tuple-element.124), channel_id=1, source_target_pairs={{0,4},{1,5},{2,6},{3,7},{4,8},{5,9},{6,10},{7,11},{8,12},{9,13},{1... | collective-permute-start | bytes 774152 | tf_op jit(solution)/shard_map/ppermute | solution.py:27
  281.0 16.0 %copy-start.11 = (bf16[128,1792]{1,0:T(8,128)(2,1)S(1)}, bf16[128,1792]{1,0:T(8,128)(2,1)}, u32[]{:S(2)}) copy-start(bf16[128,1792]{1,0:T(8,128)(2,1)} %copy-done.10) | copy-start | bytes 1376260
  281.6 17.2 %copy-start.9 = (bf16[128,1792]{1,0:T(8,128)(2,1)S(1)}, bf16[128,1792]{1,0:T(8,128)(2,1)}, u32[]{:S(2)}) copy-start(bf16[128,1792]{1,0:T(8,128)(2,1)} %copy-done.8) | copy-start | bytes 1376260
  285.2 22.7 %collective-permute-start.32 = (bf16[128,1792]{1,0:T(8,128)(2,1)S(1)}, bf16[128,1792]{1,0:T(8,128)(2,1)S(1)}, u32[]{:S(2)}, u32[]{:S(2)}) collective-permute-start(bf16[128,1792]{1,0:T(8,128)(2,1)S(1)} %shard_map.110), channel_id=1, source_target_pairs={{0,112},{16,0},{32,16},{48,32},{64,48},{80,64},{96,80},{112,96},{1... | collective-permute-start | bytes 1376264 | tf_op jit(solution)/shard_map/ppermute | solution.py:19
  296.9 20.8 %collective-permute-start.44 = (bf16[128,1792]{1,0:T(8,128)(2,1)S(1)}, bf16[128,1792]{1,0:T(8,128)(2,1)S(1)}, u32[]{:S(2)}, u32[]{:S(2)}) collective-permute-start(bf16[128,1792]{1,0:T(8,128)(2,1)S(1)} %shard_map.118), channel_id=1, source_target_pairs={{0,112},{16,0},{32,16},{48,32},{64,48},{80,64},{96,80},{112,96},{1... | collective-permute-start | bytes 1376264 | tf_op jit(solution)/shard_map/ppermute | solution.py:19
  298.7 28.9 %collective-permute-start.38 = (bf16[128,1792]{1,0:T(8,128)(2,1)S(1)}, bf16[128,1792]{1,0:T(8,128)(2,1)S(1)}, u32[]{:S(2)}, u32[]{:S(2)}) collective-permute-start(bf16[128,1792]{1,0:T(8,128)(2,1)S(1)} %shard_map.114), channel_id=1, source_target_pairs={{0,112},{16,0},{32,16},{48,32},{64,48},{80,64},{96,80},{112,96},{1... | collective-permute-start | bytes 1376264 | tf_op jit(solution)/shard_map/ppermute | solution.py:19
  300.4 33.9 %collective-permute-start.50 = (bf16[128,1792]{1,0:T(8,128)(2,1)S(1)}, bf16[128,1792]{1,0:T(8,128)(2,1)S(1)}, u32[]{:S(2)}, u32[]{:S(2)}) collective-permute-start(bf16[128,1792]{1,0:T(8,128)(2,1)S(1)} %shard_map.122), channel_id=1, source_target_pairs={{0,112},{16,0},{32,16},{48,32},{64,48},{80,64},{96,80},{112,96},{1... | collective-permute-start | bytes 1376264 | tf_op jit(solution)/shard_map/ppermute | solution.py:19
  (14 other events, 44.3 us)
